TPU v7x, 32 devices: a whole 2x2x4 slice. The times are simulated.
32 devices in a mesh: pre: 8 (over y, x, core), rep: 4 (over z).
Axes of the slice: x: 2, y: 2, z: 4, core: 2. Of those that a mesh axis runs over, the one named last changes fastest.
Arguments:
- grads: bfloat16 [8, 8, 512, 512], P('rep', 'pre')
- owner: int32 [8], replicated, may hold values from 0 to 7, as said below
- state: float32 [8, 2, 512, 512], P('pre', None, 'rep'), as said below
Outputs:
- new_state: float32 [8, 2, 512, 512], P('pre', None, 'rep')
- update: bfloat16 [8, 512, 512], P('pre', 'rep')
Inputs may be any that keep to these rules, and one draw needn't show every extreme that they name: Each owner index is named by at most 2 blocks, and some owner by exactly 2. `state`: each matrix is symmetric.
All inputs are finite; a program needn't handle non-finite values.
Results may differ from a plain program's by a relative error of at most 0.006.
Values sent between devices are 32-bit elements; how exact they have to be, the bound alone decides.
A program may use at most 64 MiB of HBM per device.

v0:
```python
import jax
import jax.numpy as jnp
from jax import lax
from jax.sharding import PartitionSpec as P

ITERS = 4


DAMP = 0.05


def inverse_root_rows(stat_rows):
    row_count = stat_rows.shape[1]
    order_size = stat_rows.shape[2]
    offset = lax.axis_index("rep") * row_count
    identity = jnp.eye(order_size, dtype=jnp.float32)
    row_ids = lax.broadcasted_iota(jnp.int32, (row_count, order_size), 0) + offset
    col_ids = lax.broadcasted_iota(jnp.int32, (row_count, order_size), 1)
    eye_rows = (row_ids == col_ids).astype(jnp.float32)
    squares = lax.psum(jnp.sum(stat_rows * stat_rows, axis=(1, 2)), "rep")
    norm_stat = jnp.sqrt(squares)
    damped = stat_rows + (DAMP * norm_stat)[:, None, None] * eye_rows
    scale_norm = jnp.sqrt(lax.psum(jnp.sum(damped * damped, axis=(1, 2)), "rep"))
    iterate = damped / scale_norm[:, None, None]
    root_rows = (scale_norm ** (-0.25))[:, None, None] * eye_rows
    for rounds in range(ITERS):
        whole_iterate = lax.all_gather(iterate, "rep", axis=1, tiled=True)
        factor = (5.0 * identity - whole_iterate) * 0.25
        root_rows = jnp.einsum("srk,skj->srj", root_rows, factor, precision=lax.Precision.HIGHEST)
        if rounds + 1 < ITERS:
            for repeat in range(4):
                iterate = jnp.einsum(
                    "srk,skj->srj", iterate, factor, precision=lax.Precision.HIGHEST
                )
    return root_rows


def body(grads, owner, state):
    local_grads = grads[:, 0]
    micro_count = local_grads.shape[0]
    capacity = state.shape[1]
    gram_rows = lax.psum_scatter(
        lax.dot_general(
            local_grads,
            local_grads,
            (((0, 2), (0, 2)), ((), ())),
            preferred_element_type=jnp.float32,
        ),
        "rep",
        scatter_dimension=0,
        tiled=True,
    )
    grad_total = lax.psum(jnp.sum(local_grads, axis=0, dtype=jnp.float32), "rep")
    mean_grad = (grad_total / (micro_count * lax.axis_size("rep"))).astype(jnp.bfloat16)
    own_index = lax.axis_index("pre")
    blocks = owner.shape[0]
    block_ids = jnp.arange(blocks, dtype=jnp.int32)
    earlier = (owner[None, :] == owner[:, None]) & (block_ids[None, :] < block_ids[:, None])
    slot_of = jnp.sum(earlier.astype(jnp.int32), axis=1)
    my_owner = owner[own_index]
    target = (block_ids == my_owner).astype(jnp.float32)
    outgoing = target[:, None, None] * gram_rows[None]
    incoming = lax.all_to_all(outgoing, "pre", split_axis=0, concat_axis=0, tiled=True)
    slot_ids = jnp.arange(capacity, dtype=jnp.int32)
    held_slots = ((owner[:, None] == own_index) & (slot_of[:, None] == slot_ids[None, :])).astype(
        jnp.float32
    )
    new_state = state[0] + jnp.einsum(
        "qs,qrk->srk", held_slots, incoming, precision=lax.Precision.HIGHEST
    )
    outbound = jnp.einsum(
        "qs,srk->qrk", held_slots, inverse_root_rows(new_state), precision=lax.Precision.HIGHEST
    )
    precond = jnp.sum(
        lax.all_to_all(outbound, "pre", split_axis=0, concat_axis=0, tiled=True), axis=0
    )
    update = jnp.dot(
        precond.astype(jnp.bfloat16), mean_grad, preferred_element_type=jnp.float32
    ).astype(jnp.bfloat16)
    return (new_state[None], update[None])


def solution(mesh):
    placed = (P("rep", "pre", None, None), P(), P("pre", None, "rep", None))
    return jax.shard_map(
        body,
        mesh=mesh,
        in_specs=placed,
        out_specs=(P("pre", None, "rep", None), P("pre", "rep", None)),
        check_vma=False,
    )
```

profile of v0, /device:TPU:0, one launch (start us, length us, event | category | flops | bytes accessed | tf_op | source)
XLA Modules:
  0.0 380.1 jit_solution(3582877834098788917)
XLA Ops:
  7.2 0.0 reduce-scatter.2.cloned.1.call-start
  7.2 3.3 convolution_bitcast_fusion
  10.6 0.0 reduce-scatter.2.cloned.1.call-update
  10.6 0.6 dynamic_slice.3
  11.2 0.6 compare_convert_fusion
  11.8 28.7 %reduce-scatter.2.cloned.1.call-done = f32[128,512]{1,0:T(8,128)} async-done(((f32[512,512]{1,0:T(8,128)}), f32[128,512]{1,0:T(8,128)}) %reduce-scatter.2.cloned.1.call-update) | async-done | bytes 262160 | tf_op jit(solution)/shard_map/reduce_scatter | solution.py:42
  40.6 2.6 broadcast_multiply_fusion
  43.2 3.7 all-to-all-start
  46.9 0.0 all-gather.5.cloned.1.call-start
  46.9 0.2 convert_reduce_fusion.1
  47.1 0.1 fusion.21
  47.2 26.3 %all-to-all-done = f32[8,128,512]{2,1,0:T(8,128)S(1)} async-done(((f32[8,128,512]{2,1,0:T(8,128)}), f32[8,128,512]{2,1,0:T(8,128)S(1)}, u32[]{:S(2)}, u32[]{:S(2)}) %all-to-all-start) | async-done | bytes 2097184 | tf_op jit(solution)/shard_map/all_to_all | solution.py:63
  73.5 2.2 fusion.6
  75.7 0.0 copy-done.10
  75.7 0.3 multiply_reduce_fusion.1
  76.0 9.4 %psum.21 = f32[2]{0:T(128)S(1)} all-reduce(f32[2]{0:T(128)S(1)} %get-tuple-element.10), channel_id=1, replica_groups=mesh['pre'=8,'rep'=4] {'rep'}, use_global_device_ids=true, to_apply=%region_3.0 | all-reduce | flops 2 | bytes 16 | tf_op jit(solution)/shard_map/psum | solution.py:20
  85.4 0.3 multiply_reduce_fusion
  85.7 9.3 %psum.22 = f32[2]{0:T(128)S(1)} all-reduce(f32[2]{0:T(128)S(1)} %multiply_reduce_fusion), channel_id=1, replica_groups=mesh['pre'=8,'rep'=4] {'rep'}, use_global_device_ids=true, to_apply=%region_5.0 | all-reduce | flops 2 | bytes 16 | tf_op jit(solution)/shard_map/psum | solution.py:23
  95.0 0.2 fusion.18
  95.2 0.8 copy-done.6
  96.0 1.2 copy.72
  97.2 0.0 all-gather.5.cloned.1.call-update
  97.2 0.0 all-gather.7.cloned.1.call-start
  97.2 0.1 fusion.12
  97.4 42.8 %all-gather.5.cloned.1.call-done = f32[2,512,512]{2,0,1:T(2,128)} async-done(((f32[2,128,512]{2,0,1:T(2,128)}), f32[2,512,512]{2,0,1:T(2,128)}) %all-gather.5.cloned.1.call-update) | async-done | bytes 2097168 | tf_op jit(solution)/shard_map/all_gather | solution.py:27
  140.2 3.5 fusion.38
  143.7 1.7 fusion.36
  145.4 1.7 fusion.34
  147.1 1.7 fusion.32
  148.8 0.8 copy-done.7
  149.6 1.2 copy.74
  150.8 0.0 all-gather.7.cloned.1.call-update
  150.8 0.2 all-gather.9.cloned.1.call-start
  151.0 44.6 %all-gather.7.cloned.1.call-done = f32[2,512,512]{2,0,1:T(2,128)} async-done(((f32[2,128,512]{2,0,1:T(2,128)}), f32[2,512,512]{2,0,1:T(2,128)}) %all-gather.7.cloned.1.call-update) | async-done | bytes 2097168 | tf_op jit(solution)/shard_map/all_gather | solution.py:27
  195.6 3.5 fusion.47
  199.2 1.7 fusion.45
  200.8 1.7 fusion.43
  202.5 1.7 fusion.41
  204.2 0.8 copy-done.8
  205.0 1.2 copy.76
  206.2 0.0 all-gather.9.cloned.1.call-update
  206.2 0.3 all-gather.11.cloned.1.call-start
  206.5 44.5 %all-gather.9.cloned.1.call-done = f32[2,512,512]{2,0,1:T(2,128)} async-done(((f32[2,128,512]{2,0,1:T(2,128)}), f32[2,512,512]{2,0,1:T(2,128)}) %all-gather.9.cloned.1.call-update) | async-done | bytes 2097168 | tf_op jit(solution)/shard_map/all_gather | solution.py:27
  251.0 3.5 fusion.57
  254.6 1.7 fusion.55
  256.3 1.7 fusion.53
  258.0 1.7 fusion.51
  259.6 1.2 copy.78
  260.9 0.0 all-gather.11.cloned.1.call-update
  260.9 1.7 fusion.16
  262.6 1.7 fusion.49
  264.3 1.7 fusion.59
  265.9 39.8 %all-gather.11.cloned.1.call-done = f32[2,512,512]{2,0,1:T(2,128)} async-done(((f32[2,128,512]{2,0,1:T(2,128)}), f32[2,512,512]{2,0,1:T(2,128)}) %all-gather.11.cloned.1.call-update) | async-done | bytes 2097168 | tf_op jit(solution)/shard_map/all_gather | solution.py:27
  305.7 3.5 fusion.1
  309.2 1.5 fusion.13
  310.7 2.6 copy.81
  313.3 3.8 all-to-all-start.1
  317.0 0.0 all-reduce.2.cloned.1.call-start
  317.1 1.2 convert_reduce_fusion
  318.3 0.0 all-reduce.2.cloned.1.call-update
  318.3 25.4 %all-to-all-done.1 = f32[8,128,512]{2,1,0:T(8,128)S(1)} async-done(((f32[8,128,512]{2,1,0:T(8,128)}), f32[8,128,512]{2,1,0:T(8,128)S(1)}, u32[]{:S(2)}, u32[]{:S(2)}) %all-to-all-start.1) | async-done | bytes 2097184 | tf_op jit(solution)/shard_map/all_to_all | solution.py:75
  343.7 0.2 reduce_sum.48
  343.9 27.3 %all-reduce.2.cloned.1.call-done = f32[512,512]{1,0:T(8,128)} async-done(((f32[512,512]{1,0:T(8,128)}), f32[512,512]{1,0:T(8,128)}) %all-reduce.2.cloned.1.call-update) | async-done | bytes 1048592 | tf_op jit(solution)/shard_map/psum | solution.py:53
  371.2 2.1 fusion.8
  (24 shorter events, 0.1 us)
Async XLA Ops:
  7.2 3.4 copy-start.11
  7.2 33.4 %reduce-scatter.2.cloned.1.call-start = ((), (), s32[]{:S(2)}) async-start(), calls=%async_computation.3 | async-start | bytes 1310720 | tf_op jit(solution)/shard_map/reduce_scatter | solution.py:42
  43.2 30.3 %all-to-all-start = ((f32[8,128,512]{2,1,0:T(8,128)}), f32[8,128,512]{2,1,0:T(8,128)S(1)}, u32[]{:S(2)}, u32[]{:S(2)}) async-start(f32[8,128,512]{2,1,0:T(8,128)} %broadcast_multiply_fusion), calls=%async_computation.1 | async-start | bytes 4194304 | tf_op jit(solution)/shard_map/all_to_all | solution.py:63
  46.9 28.8 %copy-start.10 = (f32[1,2,128,512]{3,2,1,0:T(8,128)S(1)}, f32[1,2,128,512]{3,2,1,0:T(8,128)}, u32[]{:S(2)}) copy-start(f32[1,2,128,512]{3,2,1,0:T(8,128)} %param.5) | copy-start | bytes 1572868
  46.9 93.3 %all-gather.5.cloned.1.call-start = ((), (), s32[]{:S(2)}) async-start(), calls=%async_computation.4 | async-start | bytes 2621440 | tf_op jit(solution)/shard_map/all_gather | solution.py:27
  76.0 21.2 %copy-start.5 = (f32[2,128,512]{2,1,0:T(8,128)}, f32[2,128,512]{2,1,0:T(8,128)S(1)}, u32[]{:S(2)}) copy-start(f32[2,128,512]{2,1,0:T(8,128)S(1)} %get-tuple-element.11) | copy-start | bytes 1572868
  95.1 0.8 copy-start.6
  97.2 98.4 %all-gather.7.cloned.1.call-start = ((), (), s32[]{:S(2)}) async-start(), calls=%async_computation.5 | async-start | bytes 2621440 | tf_op jit(solution)/shard_map/all_gather | solution.py:27
  140.2 3.6 copy-start
  148.8 0.8 copy-start.7
  150.8 100.2 %all-gather.9.cloned.1.call-start = ((), (), s32[]{:S(2)}) async-start(), calls=%async_computation.6 | async-start | bytes 2621440 | tf_op jit(solution)/shard_map/all_gather | solution.py:27
  195.6 3.6 copy-start.1
  204.2 0.8 copy-start.8
  206.2 99.5 %all-gather.11.cloned.1.call-start = ((), (), s32[]{:S(2)}) async-start(), calls=%async_computation.7 | async-start | bytes 2621440 | tf_op jit(solution)/shard_map/all_gather | solution.py:27
  251.0 3.6 copy-start.3
  260.9 1.7 copy-start.2
  262.6 1.7 copy-start.4
  313.3 3.8 %copy-start.9 = (bf16[2,1,512,512]{3,2,1,0:T(8,128)(2,1)S(1)}, bf16[2,1,512,512]{3,2,1,0:T(8,128)(2,1)}, u32[]{:S(2)}) copy-start(bf16[2,1,512,512]{3,2,1,0:T(8,128)(2,1)} %param.3) | copy-start | bytes 3145732
  313.3 30.4 %all-to-all-start.1 = ((f32[8,128,512]{2,1,0:T(8,128)}), f32[8,128,512]{2,1,0:T(8,128)S(1)}, u32[]{:S(2)}, u32[]{:S(2)}) async-start(f32[8,128,512]{2,1,0:T(8,128)} %copy.81), calls=%async_computation.2 | async-start | bytes 4194304 | tf_op jit(solution)/shard_map/all_to_all | solution.py:75
  317.0 54.1 %all-reduce.2.cloned.1.call-start = ((), (), s32[]{:S(2)}) async-start(), calls=%async_computation.8 | async-start | bytes 2097152 | tf_op jit(solution)/shard_map/psum | solution.py:53
Sparse Core Ops, SparseCore 0:
  10.7 29.8 reduce-scatter.1
  97.3 42.8 all-gather.4
  150.9 44.6 all-gather.6
  206.3 44.6 all-gather.8
  261.0 44.6 all-gather.10
  320.0 51.0 all-reduce.1
where the time goes:
time: 381 us; the launch traced here: 380 us
  waiting for transfers between devices  279 us (73%)
  matrix products  43.3 us (11%)
  blocking collectives  18.7 us (5%)
  between operations  14.4 us (4%)
  local copies, waits for them, and re-layouts  10.4 us (3%)
  starting transfers between devices  8.05 us (2%)
  other arithmetic  5.75 us (2%)
    all_gather x4, waiting for transfers between devices, inverse_root_rows(): whole_iterate = lax.all_gather(iterate, 'rep', axis=1, tiled=True)  172 us
    reduce_scatter x1, waiting for transfers between devices, body(): lax.psum_scatter(lax.dot_general(local_grads, local_grads, (((0, 2), (0,...  28.7 us
    psum x1, waiting for transfers between devices, body(): lax.psum(jnp.sum(local_grads, axis=0, dtype=jnp.float32), 'rep')  27.3 us
    all_to_all x1, waiting for transfers between devices, body(): lax.all_to_all(outgoing, 'pre', split_axis=0, concat_axis=0, tiled=True)  26.3 us
    dot_general x12, matrix products, inverse_root_rows(): jnp.einsum('srk,skj->srj', iterate, factor, precision=lax.Precision.HIGHEST)  25.6 us
    all_to_all x1, waiting for transfers between devices, body(): lax.all_to_all(outbound, 'pre', split_axis=0, concat_axis=0, tiled=True)  25.4 us
    psum x1, blocking collectives, inverse_root_rows(): squares = lax.psum(jnp.sum(stat_rows * stat_rows, axis=(1, 2)), 'rep')  9.42 us
    psum x1, blocking collectives, inverse_root_rows(): lax.psum(jnp.sum(damped * damped, axis=(1, 2)), 'rep')  9.27 us
  transfers between devices with their start and end apart: 8, of which 8 were waited for; matrix products, arithmetic and copies ran while one was open for 2% of the time, Pallas kernels for 0%

commit v1 on v0

v1 whole, which is shorter than its diff:
```python
import functools

import jax
import jax.numpy as jnp
from jax import lax
from jax.experimental import pallas as pl
from jax.experimental.pallas import tpu as pltpu
from jax.sharding import PartitionSpec as P

DAMP = 0.05
LANES = 128
LAG = 2
CENTER = 1.5625


def nt_dot(a, b):
    return lax.dot_general(a, b, (((1,), (1,)), ((), ())), preferred_element_type=jnp.float32)


def dot(a, b):
    return jnp.dot(a, b, preferred_element_type=jnp.float32)


def kernel(
    n_pre,
    n_rep,
    owner_ref,
    grads_ref,
    state_ref,
    new_state_ref,
    update_ref,
    loc,
    up,
    dn,
    tot,
    route_out,
    route_in,
    rows_in,
    stat,
    mean,
    x_f32,
    x_b16,
    e_f32,
    e_b16,
    g_b16,
    in_send,
    out_send,
    up_recv,
    dn_recv,
    route_send,
    route_recv,
    rows_send,
    rows_recv,
):
    pre, rep = lax.axis_index("pre"), lax.axis_index("rep")
    shards, order = grads_ref.shape[0], grads_ref.shape[2]
    rows, capacity = state_ref.shape[2], state_ref.shape[1]
    blocks = order // LANES
    half = n_rep // 2
    is_end = (rep == 0) | (rep == n_rep - 1)
    is_mid = (rep == half - 1) | (rep == half)
    not_end, not_mid = jnp.logical_not(is_end), jnp.logical_not(is_mid)
    inward = jnp.where(rep < half, rep + 1, rep - 1)
    outward = jnp.where(rep < half, rep - 1, rep + 1)

    mean_tiles = [(i, j) for i in range(n_rep) for j in range(blocks)]
    stat_tiles = [(i, j) for i in range(n_rep) for j in range(i * rows // LANES, blocks)]
    n_mean, total = len(mean_tiles), len(mean_tiles) + len(stat_tiles)

    def remote(src, dst, send, recv, device):
        return pltpu.make_async_remote_copy(
            src_ref=src,
            dst_ref=dst,
            send_sem=send,
            recv_sem=recv,
            device_id=device,
            device_id_type=pl.DeviceIdType.MESH,
        )

    barrier = pltpu.get_barrier_semaphore()

    @pl.loop(1, n_pre)
    def _(step):
        pl.semaphore_signal(
            barrier,
            inc=1,
            device_id={"pre": lax.rem(pre + step, n_pre)},
            device_id_type=pl.DeviceIdType.MESH,
        )

    pl.semaphore_signal(
        barrier, inc=1, device_id={"rep": inward}, device_id_type=pl.DeviceIdType.MESH
    )

    @pl.when(not_end)
    def _():
        pl.semaphore_signal(
            barrier, inc=1, device_id={"rep": outward}, device_id_type=pl.DeviceIdType.MESH
        )

    pl.semaphore_wait(barrier, jnp.where(is_end, n_pre, n_pre + 1))

    def slot_of(block):
        mine = owner_ref[block]

        def count(other, found):
            same = (owner_ref[other] == mine) & (other < block)
            return found + same.astype(jnp.int32)

        return lax.fori_loop(0, n_pre, count, jnp.int32(0))

    def piece(block):
        return state_ref[0, jnp.minimum(slot_of(block), capacity - 1)]

    def route_copy(step):
        peer = lax.rem(pre + step, n_pre)
        return remote(
            route_out.at[step],
            route_in.at[pre],
            route_send.at[step],
            route_recv.at[step],
            {"pre": peer},
        )

    @pl.loop(1, n_pre)
    def _(step):
        route_out[step] = piece(lax.rem(pre + step, n_pre))
        route_copy(step).start()

    route_in[pre] = piece(pre)

    def send_in(k):
        @pl.when(is_mid)
        def _():
            remote(
                loc.at[k], dn.at[k], in_send.at[k], dn_recv.at[k], {"rep": inward}
            ).start()

        @pl.when(not_mid)
        def _():
            remote(
                loc.at[k], up.at[k], in_send.at[k], up_recv.at[k], {"rep": inward}
            ).start()

    def out_copy(k):
        return remote(tot.at[k], dn.at[k], out_send.at[k], dn_recv.at[k], {"rep": outward})

    def in_copy(k):
        return remote(loc.at[k], up.at[k], in_send.at[k], up_recv.at[k], {"rep": inward})

    def step_up(k):
        @pl.when(not_end)
        def _():
            in_copy(k).wait_recv()
            loc[k] = loc[k] + up[k]
            send_in(k)

    def step_down(k):
        out_copy(k).wait_recv()

        @pl.when(is_mid)
        def _():
            tot[k] = loc[k] + dn[k]

        @pl.when(not_mid)
        def _():
            tot[k] = dn[k]

        @pl.when(not_end)
        def _():
            out_copy(k).start()

    for k, (i, j) in enumerate(mean_tiles):
        r, c = slice(i * rows, (i + 1) * rows), slice(j * LANES, (j + 1) * LANES)
        acc = grads_ref[0, 0, r, c].astype(jnp.float32)
        for s in range(1, shards):
            acc = acc + grads_ref[s, 0, r, c].astype(jnp.float32)
        loc[k] = acc

        @pl.when(is_end)
        def _():
            send_in(k)

    for a in range(blocks):
        low = a * LANES
        gram = nt_dot(grads_ref[0, 0, low : low + LANES, :], grads_ref[0, 0, low:, :])
        for s in range(1, shards):
            gram = gram + nt_dot(grads_ref[s, 0, low : low + LANES, :], grads_ref[s, 0, low:, :])
        for k, (i, j) in enumerate(stat_tiles):
            if i * rows // LANES == a:
                r = i * rows - low
                loc[n_mean + k] = gram[r : r + rows, j * LANES - low : (j + 1) * LANES - low]

    def inject():
        @pl.loop(1, n_pre)
        def _(step):
            route_copy(step).wait_recv()

        held = route_in[owner_ref[pre]]
        for k, (i, j) in enumerate(stat_tiles):

            @pl.when(rep == i)
            def _():
                loc[n_mean + k] = loc[n_mean + k] + held[:, j * LANES : (j + 1) * LANES]

    @pl.when(is_end)
    def _():
        inject()

        @pl.loop(n_mean, total)
        def _(k):
            send_in(k)

    @pl.loop(0, LAG)
    def _(k):
        step_up(k)

    @pl.loop(LAG, n_mean)
    def _(k):
        step_up(k)
        step_down(k - LAG)

    @pl.when(not_end)
    def _():
        inject()

    @pl.loop(n_mean, total)
    def _(k):
        step_up(k)
        step_down(k - LAG)

    @pl.loop(total - LAG, total)
    def _(k):
        step_down(k)

    for k, (i, j) in enumerate(stat_tiles):
        stat[i * rows : (i + 1) * rows, j * LANES : (j + 1) * LANES] = tot[n_mean + k]
    for a in range(blocks):
        for b in range(a + 1, blocks):
            ra, rb = slice(a * LANES, (a + 1) * LANES), slice(b * LANES, (b + 1) * LANES)
            stat[rb, ra] = stat[ra, rb].T

    start = pl.multiple_of(rep * rows, rows)

    def rows_copy(step):
        peer = lax.rem(pre + step, n_pre)
        return remote(
            stat.at[pl.ds(start, rows)],
            rows_in.at[pre],
            rows_send.at[step],
            rows_recv.at[step],
            {"pre": peer},
        )

    @pl.loop(1, n_pre)
    def _(step):
        rows_copy(step).start()

    rows_in[pre] = stat[pl.ds(start, rows), :]

    for k, (i, j) in enumerate(mean_tiles):
        mean[i * rows : (i + 1) * rows, j * LANES : (j + 1) * LANES] = (
            tot[k] / (shards * n_rep)
        ).astype(jnp.bfloat16)

    def eye(first, count):
        r = lax.broadcasted_iota(jnp.int32, (count, order), 0) + first
        c = lax.broadcasted_iota(jnp.int32, (count, order), 1)
        return (r == c).astype(jnp.float32)

    bands = range(0, order, 256)
    squares = jnp.zeros((1, 1), jnp.float32)
    for b in bands:
        part = stat[b : b + 256, :]
        squares = squares + jnp.sum(part * part, keepdims=True)
    shift = DAMP * jnp.sqrt(squares)
    squares = jnp.zeros((1, 1), jnp.float32)
    for b in bands:
        part = stat[b : b + 256, :] + shift * eye(b, 256)
        x_f32[b : b + 256, :] = part
        squares = squares + jnp.sum(part * part, keepdims=True)
    scale = jnp.sqrt(squares)
    for b in bands:
        part = x_f32[b : b + 256, :] / scale
        x_f32[b : b + 256, :] = part
        x_b16[b : b + 256, :] = part.astype(jnp.bfloat16)
    root = (1.25 * eye(start, rows) - 0.25 * x_f32[pl.ds(start, rows), :]) / jnp.sqrt(
        jnp.sqrt(scale)
    )

    def quadratic(b):
        square = dot(x_b16[pl.ds(b, 256), :], x_b16[...])
        return 0.0625 * square - 0.625 * x_f32[pl.ds(b, 256), :]

    @pl.loop(0, 2, init_carry=root)
    def root(_, root):
        @pl.loop(0, order, step=256)
        def _(b):
            e = quadratic(b)
            e_f32[pl.ds(b, 256), :] = e
            e_b16[pl.ds(b, 256), :] = e.astype(jnp.bfloat16)

        @pl.loop(0, order, step=256)
        def _(b):
            g = 2.0 * CENTER * e_f32[pl.ds(b, 256), :] + dot(e_b16[pl.ds(b, 256), :], e_b16[...])
            g_b16[pl.ds(b, 256), :] = g.astype(jnp.bfloat16)

        @pl.loop(0, order, step=256)
        def _(b):
            x = CENTER * CENTER * x_f32[pl.ds(b, 256), :] + dot(
                x_b16[pl.ds(b, 256), :], g_b16[...]
            )
            x_f32[pl.ds(b, 256), :] = x
            x_b16[pl.ds(b, 256), :] = x.astype(jnp.bfloat16)

        return 1.25 * root - 0.25 * dot(root.astype(jnp.bfloat16), x_b16[...])

    @pl.loop(0, order, step=256)
    def _(b):
        e_b16[pl.ds(b, 256), :] = quadratic(b).astype(jnp.bfloat16)

    last = dot(root.astype(jnp.bfloat16), x_b16[...])
    for _ in range(2):
        last = CENTER * last + dot(last.astype(jnp.bfloat16), e_b16[...])
    precond = (1.25 * root - 0.25 * last).astype(jnp.bfloat16)
    update_ref[0] = dot(precond, mean[...]).astype(jnp.bfloat16)

    @pl.loop(1, n_pre)
    def _(step):
        rows_copy(step).wait_recv()

    for j in range(capacity):

        def find(block, found):
            has, at = found
            here = ((owner_ref[block] == pre) & (slot_of(block) == j)).astype(jnp.int32)
            return has + here, at + here * block

        has, at = lax.fori_loop(0, n_pre, find, (jnp.int32(0), jnp.int32(0)))
        taken = jnp.full((rows, order), has, jnp.int32) > 0
        new_state_ref[0, j] = jnp.where(taken, rows_in[at], state_ref[0, j])

    @pl.loop(1, n_pre)
    def _(step):
        route_copy(step).wait_send()
        rows_copy(step).wait_send()

    @pl.loop(0, total)
    def _(k):
        in_copy(k).wait_send()

        @pl.when(not_end)
        def _():
            out_copy(k).wait_send()


def body(n_pre, n_rep, grads, owner, state):
    order = grads.shape[2]
    rows = state.shape[2]
    blocks = order // LANES
    total = n_rep * blocks + sum(blocks - i * rows // LANES for i in range(n_rep))
    f32, b16 = jnp.float32, jnp.bfloat16
    dma = pltpu.SemaphoreType.DMA
    vmem = pl.BlockSpec(memory_space=pltpu.VMEM)
    return pl.pallas_call(
        functools.partial(kernel, n_pre, n_rep),
        out_shape=(
            jax.ShapeDtypeStruct(state.shape, f32),
            jax.ShapeDtypeStruct((1, rows, order), b16),
        ),
        in_specs=[pl.BlockSpec(memory_space=pltpu.SMEM), vmem, vmem],
        out_specs=(vmem, vmem),
        scratch_shapes=[pltpu.VMEM((total, rows, LANES), f32)] * 4
        + [pltpu.VMEM((n_pre, rows, order), f32)] * 3
        + [pltpu.VMEM((order, order), t) for t in (f32, b16, f32, b16, f32, b16, b16)]
        + [dma((total,))] * 4
        + [dma((n_pre,))] * 4,
        compiler_params=pltpu.CompilerParams(
            collective_id=0, has_side_effects=True, vmem_limit_bytes=40 * 1024 * 1024
        ),
        cost_estimate=pl.CostEstimate(
            flops=20 * order**3, bytes_accessed=4 * order * order * 4, transcendentals=0
        ),
    )(owner, grads, state)


def solution(mesh):
    placed = (P("rep", "pre", None, None), P(), P("pre", None, "rep", None))
    return jax.shard_map(
        functools.partial(body, mesh.shape["pre"], mesh.shape["rep"]),
        mesh=mesh,
        in_specs=placed,
        out_specs=(P("pre", None, "rep", None), P("pre", "rep", None)),
        check_vma=False,
    )
```

time: 381 us -> 83.7 us (0.22)
  the two profiles are of different devices: /device:TPU:0 before, /device:TPU:1 now
where the time goes in v1:
time: 83.7 us; the launch traced here: 83.5 us
  Pallas kernels  78.5 us (94%)
  local copies, waits for them, and re-layouts  4.36 us (5%)
    pallas_call x1, Pallas kernels, body(): pl.pallas_call(functools.partial(kernel, n_pre, n_rep), out_shape=(jax.Sh...  78.5 us
    unnamed x8, local copies, waits for them, and re-layouts  4.36 us

profile of v1, /device:TPU:1, one launch (start us, length us, event | category | flops | bytes accessed | tf_op | source)
XLA Modules:
  0.0 83.5 jit_solution(14559364654635771665)
XLA Ops:
  0.6 0.0 copy-start
  0.6 1.2 %copy-done = bf16[2,1,512,512]{3,2,1,0:T(8,128)(2,1)S(1)} copy-done((bf16[2,1,512,512]{3,2,1,0:T(8,128)(2,1)S(1)}, bf16[2,1,512,512]{3,2,1,0:T(8,128)(2,1)}, u32[]{:S(2)}) %copy-start) | copy-done | bytes 1048600
  1.9 0.0 copy-start.1
  1.9 1.0 %copy-done.1 = f32[1,2,128,512]{3,2,1,0:T(8,128)S(1)} copy-done((f32[1,2,128,512]{3,2,1,0:T(8,128)S(1)}, f32[1,2,128,512]{3,2,1,0:T(8,128)}, u32[]{:S(2)}) %copy-start.1) | copy-done | bytes 524312
  2.9 0.0 copy-start.2
  2.9 0.7 copy-done.2
  3.6 78.5 %shard_map.50 = (f32[1,2,128,512]{3,2,1,0:T(8,128)S(1)}, bf16[1,128,512]{2,1,0:T(8,128)(2,1)S(1)}) custom-call(s32[8]{0:T(128)S(1)} %copy-done.2, bf16[2,1,512,512]{3,2,1,0:T(8,128)(2,1)S(1)} %copy-done, f32[1,2,128,512]{3,2,1,0:T(8,128)S(1)} %copy-done.1), custom_call_target="tpu_custom_call" | custom-call | flops 2684354560 | bytes 4194304 | tf_op jit(solution)/shard_map/pallas_call | solution.py:365
  82.1 0.8 copy.7
  82.9 0.7 copy.8
Async XLA Ops:
  0.6 1.2 %copy-start = (bf16[2,1,512,512]{3,2,1,0:T(8,128)(2,1)S(1)}, bf16[2,1,512,512]{3,2,1,0:T(8,128)(2,1)}, u32[]{:S(2)}) copy-start(bf16[2,1,512,512]{3,2,1,0:T(8,128)(2,1)} %grads_ref.1) | copy-start | bytes 3145732
  1.9 1.0 %copy-start.1 = (f32[1,2,128,512]{3,2,1,0:T(8,128)S(1)}, f32[1,2,128,512]{3,2,1,0:T(8,128)}, u32[]{:S(2)}) copy-start(f32[1,2,128,512]{3,2,1,0:T(8,128)} %state_ref.1) | copy-start | bytes 1572868
  2.9 0.7 copy-start.2

commit v2 on v1

--- a/solution.py
+++ b/solution.py
@@ -9,7 +9,7 @@
 
 DAMP = 0.05
 LANES = 128
-LAG = 2
+LAG = 3
 CENTER = 1.5625
 
 
@@ -33,6 +33,8 @@
     up,
     dn,
     tot,
+    core_out,
+    core_in,
     route_out,
     route_in,
     rows_in,
@@ -47,10 +49,14 @@
     out_send,
     up_recv,
     dn_recv,
+    core_send,
+    core_recv,
     route_send,
     route_recv,
     rows_send,
     rows_recv,
+    pass_send,
+    pass_recv,
 ):
     pre, rep = lax.axis_index("pre"), lax.axis_index("rep")
     shards, order = grads_ref.shape[0], grads_ref.shape[2]
@@ -62,10 +68,25 @@
     not_end, not_mid = jnp.logical_not(is_end), jnp.logical_not(is_mid)
     inward = jnp.where(rep < half, rep + 1, rep - 1)
     outward = jnp.where(rep < half, rep - 1, rep + 1)
+    chips, chip, core = n_pre // 2, pre // 2, pre % 2
+    partner = pre + 1 - 2 * core
+
+    def chip_at(d):
+        other, bit = chip, 1
+        while bit < chips:
+            if d & bit:
+                other = other + bit * (1 - 2 * ((chip // bit) % 2))
+            bit *= 2
+        return other
 
     mean_tiles = [(i, j) for i in range(n_rep) for j in range(blocks)]
     stat_tiles = [(i, j) for i in range(n_rep) for j in range(i * rows // LANES, blocks)]
-    n_mean, total = len(mean_tiles), len(mean_tiles) + len(stat_tiles)
+    early = len(mean_tiles) // 2
+    after = early + len(stat_tiles)
+    total = len(mean_tiles) + len(stat_tiles)
+
+    def mean_place(k):
+        return k if k < early else k + len(stat_tiles)
 
     def remote(src, dst, send, recv, device):
         return pltpu.make_async_remote_copy(
@@ -79,55 +100,21 @@
 
     barrier = pltpu.get_barrier_semaphore()
 
-    @pl.loop(1, n_pre)
-    def _(step):
+    def greet(device):
         pl.semaphore_signal(
-            barrier,
-            inc=1,
-            device_id={"pre": lax.rem(pre + step, n_pre)},
-            device_id_type=pl.DeviceIdType.MESH,
+            barrier, inc=1, device_id=device, device_id_type=pl.DeviceIdType.MESH
         )
 
-    pl.semaphore_signal(
-        barrier, inc=1, device_id={"rep": inward}, device_id_type=pl.DeviceIdType.MESH
-    )
+    for d in range(1, chips):
+        greet({"pre": 2 * chip_at(d) + core})
+    greet({"pre": partner})
+    greet({"rep": inward})
 
     @pl.when(not_end)
     def _():
-        pl.semaphore_signal(
-            barrier, inc=1, device_id={"rep": outward}, device_id_type=pl.DeviceIdType.MESH
-        )
-
-    pl.semaphore_wait(barrier, jnp.where(is_end, n_pre, n_pre + 1))
-
-    def slot_of(block):
-        mine = owner_ref[block]
-
-        def count(other, found):
-            same = (owner_ref[other] == mine) & (other < block)
-            return found + same.astype(jnp.int32)
-
-        return lax.fori_loop(0, n_pre, count, jnp.int32(0))
-
-    def piece(block):
-        return state_ref[0, jnp.minimum(slot_of(block), capacity - 1)]
-
-    def route_copy(step):
-        peer = lax.rem(pre + step, n_pre)
-        return remote(
-            route_out.at[step],
-            route_in.at[pre],
-            route_send.at[step],
-            route_recv.at[step],
-            {"pre": peer},
-        )
-
-    @pl.loop(1, n_pre)
-    def _(step):
-        route_out[step] = piece(lax.rem(pre + step, n_pre))
-        route_copy(step).start()
-
-    route_in[pre] = piece(pre)
+        greet({"rep": outward})
+
+    pl.semaphore_wait(barrier, jnp.where(is_end, chips + 1, chips + 2))
 
     def send_in(k):
         @pl.when(is_mid)
@@ -175,11 +162,43 @@
         acc = grads_ref[0, 0, r, c].astype(jnp.float32)
         for s in range(1, shards):
             acc = acc + grads_ref[s, 0, r, c].astype(jnp.float32)
-        loc[k] = acc
-
-        @pl.when(is_end)
-        def _():
-            send_in(k)
+        loc[mean_place(k)] = acc
+        if k < early:
+
+            @pl.when(is_end)
+            def _():
+                send_in(k)
+
+    def slot_of(block):
+        mine = owner_ref[block]
+
+        def count(other, found):
+            same = (owner_ref[other] == mine) & (other < block)
+            return found + same.astype(jnp.int32)
+
+        return lax.fori_loop(0, n_pre, count, jnp.int32(0))
+
+    def piece(block):
+        return state_ref[0, jnp.minimum(slot_of(block), capacity - 1)]
+
+    def core_copy(d):
+        return remote(
+            core_out.at[d], core_in.at[d], core_send.at[d], core_recv.at[d], {"pre": partner}
+        )
+
+    def route_copy(d):
+        return remote(
+            route_out.at[d],
+            route_in.at[chip],
+            route_send.at[d],
+            route_recv.at[d],
+            {"pre": 2 * chip_at(d) + core},
+        )
+
+    far_first = list(range(chips - 1, -1, -1))
+    for d in far_first:
+        core_out[d] = piece(2 * chip_at(d) + 1 - core)
+        core_copy(d).start()
 
     for a in range(blocks):
         low = a * LANES
@@ -189,25 +208,34 @@
         for k, (i, j) in enumerate(stat_tiles):
             if i * rows // LANES == a:
                 r = i * rows - low
-                loc[n_mean + k] = gram[r : r + rows, j * LANES - low : (j + 1) * LANES - low]
+                loc[early + k] = gram[r : r + rows, j * LANES - low : (j + 1) * LANES - low]
+
+    for d in far_first:
+        block = 2 * chip_at(d) + core
+        core_copy(d).wait_recv()
+        theirs = jnp.full((rows, order), (owner_ref[block] == partner).astype(jnp.int32)) > 0
+        chosen = jnp.where(theirs, core_in[d], piece(block))
+        if d:
+            route_out[d] = chosen
+            route_copy(d).start()
+        else:
+            route_in[chip] = chosen
 
     def inject():
-        @pl.loop(1, n_pre)
-        def _(step):
-            route_copy(step).wait_recv()
-
-        held = route_in[owner_ref[pre]]
+        for d in range(1, chips):
+            route_copy(d).wait_recv()
+        held = route_in[owner_ref[pre] // 2]
         for k, (i, j) in enumerate(stat_tiles):
 
             @pl.when(rep == i)
             def _():
-                loc[n_mean + k] = loc[n_mean + k] + held[:, j * LANES : (j + 1) * LANES]
+                loc[early + k] = loc[early + k] + held[:, j * LANES : (j + 1) * LANES]
 
     @pl.when(is_end)
     def _():
         inject()
 
-        @pl.loop(n_mean, total)
+        @pl.loop(early, total)
         def _(k):
             send_in(k)
 
@@ -215,7 +243,7 @@
     def _(k):
         step_up(k)
 
-    @pl.loop(LAG, n_mean)
+    @pl.loop(LAG, early)
     def _(k):
         step_up(k)
         step_down(k - LAG)
@@ -224,17 +252,20 @@
     def _():
         inject()
 
-    @pl.loop(n_mean, total)
+    @pl.loop(early, after + LAG)
     def _(k):
         step_up(k)
         step_down(k - LAG)
 
-    @pl.loop(total - LAG, total)
-    def _(k):
-        step_down(k)
+    def pump(part, parts=10):
+        left = total - after
+        for k in range(left * part // parts, left * (part + 1) // parts):
+            if after + LAG + k < total:
+                step_up(after + LAG + k)
+            step_down(after + k)
 
     for k, (i, j) in enumerate(stat_tiles):
-        stat[i * rows : (i + 1) * rows, j * LANES : (j + 1) * LANES] = tot[n_mean + k]
+        stat[i * rows : (i + 1) * rows, j * LANES : (j + 1) * LANES] = tot[early + k]
     for a in range(blocks):
         for b in range(a + 1, blocks):
             ra, rb = slice(a * LANES, (a + 1) * LANES), slice(b * LANES, (b + 1) * LANES)
@@ -242,26 +273,29 @@
 
     start = pl.multiple_of(rep * rows, rows)
 
-    def rows_copy(step):
-        peer = lax.rem(pre + step, n_pre)
+    def rows_copy(d):
+        device = {"pre": 2 * chip_at(d) + core} if d else {"pre": partner}
         return remote(
             stat.at[pl.ds(start, rows)],
             rows_in.at[pre],
-            rows_send.at[step],
-            rows_recv.at[step],
-            {"pre": peer},
+            rows_send.at[d],
+            rows_recv.at[d],
+            device,
         )
 
-    @pl.loop(1, n_pre)
-    def _(step):
-        rows_copy(step).start()
-
+    def pass_copy(d):
+        held = rows_in.at[2 * chip_at(d) + core]
+        return remote(held, held, pass_send.at[d], pass_recv.at[d], {"pre": partner})
+
+    def pass_on(d):
+        rows_copy(d).wait_recv()
+        pass_copy(d).start()
+
+    for d in range(1, chips):
+        rows_copy(d).start()
+    rows_copy(0).start()
     rows_in[pre] = stat[pl.ds(start, rows), :]
-
-    for k, (i, j) in enumerate(mean_tiles):
-        mean[i * rows : (i + 1) * rows, j * LANES : (j + 1) * LANES] = (
-            tot[k] / (shards * n_rep)
-        ).astype(jnp.bfloat16)
+    pump(0)
 
     def eye(first, count):
         r = lax.broadcasted_iota(jnp.int32, (count, order), 0) + first
@@ -280,6 +314,7 @@
         x_f32[b : b + 256, :] = part
         squares = squares + jnp.sum(part * part, keepdims=True)
     scale = jnp.sqrt(squares)
+    pump(1)
     for b in bands:
         part = x_f32[b : b + 256, :] / scale
         x_f32[b : b + 256, :] = part
@@ -287,23 +322,28 @@
     root = (1.25 * eye(start, rows) - 0.25 * x_f32[pl.ds(start, rows), :]) / jnp.sqrt(
         jnp.sqrt(scale)
     )
+    pump(2)
 
     def quadratic(b):
         square = dot(x_b16[pl.ds(b, 256), :], x_b16[...])
         return 0.0625 * square - 0.625 * x_f32[pl.ds(b, 256), :]
 
-    @pl.loop(0, 2, init_carry=root)
-    def root(_, root):
+    for turn in range(2):
+
         @pl.loop(0, order, step=256)
         def _(b):
             e = quadratic(b)
             e_f32[pl.ds(b, 256), :] = e
             e_b16[pl.ds(b, 256), :] = e.astype(jnp.bfloat16)
 
+        pump(3 + 3 * turn)
+
         @pl.loop(0, order, step=256)
         def _(b):
             g = 2.0 * CENTER * e_f32[pl.ds(b, 256), :] + dot(e_b16[pl.ds(b, 256), :], e_b16[...])
             g_b16[pl.ds(b, 256), :] = g.astype(jnp.bfloat16)
+
+        pump(4 + 3 * turn)
 
         @pl.loop(0, order, step=256)
         def _(b):
@@ -313,7 +353,11 @@
             x_f32[pl.ds(b, 256), :] = x
             x_b16[pl.ds(b, 256), :] = x.astype(jnp.bfloat16)
 
-        return 1.25 * root - 0.25 * dot(root.astype(jnp.bfloat16), x_b16[...])
+        root = 1.25 * root - 0.25 * dot(root.astype(jnp.bfloat16), x_b16[...])
+        pump(5 + 3 * turn)
+
+    for d in range(1, chips - 1):
+        pass_on(d)
 
     @pl.loop(0, order, step=256)
     def _(b):
@@ -323,11 +367,18 @@
     for _ in range(2):
         last = CENTER * last + dot(last.astype(jnp.bfloat16), e_b16[...])
     precond = (1.25 * root - 0.25 * last).astype(jnp.bfloat16)
+    pump(9)
+    pass_on(chips - 1)
+
+    for k, (i, j) in enumerate(mean_tiles):
+        mean[i * rows : (i + 1) * rows, j * LANES : (j + 1) * LANES] = (
+            tot[mean_place(k)] / (shards * n_rep)
+        ).astype(jnp.bfloat16)
     update_ref[0] = dot(precond, mean[...]).astype(jnp.bfloat16)
 
-    @pl.loop(1, n_pre)
-    def _(step):
-        rows_copy(step).wait_recv()
+    rows_copy(0).wait_recv()
+    for d in range(1, chips):
+        pass_copy(d).wait_recv()
 
     for j in range(capacity):
 
@@ -340,10 +391,12 @@
         taken = jnp.full((rows, order), has, jnp.int32) > 0
         new_state_ref[0, j] = jnp.where(taken, rows_in[at], state_ref[0, j])
 
-    @pl.loop(1, n_pre)
-    def _(step):
-        route_copy(step).wait_send()
-        rows_copy(step).wait_send()
+    for d in range(chips):
+        core_copy(d).wait_send()
+        rows_copy(d).wait_send()
+        if d:
+            route_copy(d).wait_send()
+            pass_copy(d).wait_send()
 
     @pl.loop(0, total)
     def _(k):
@@ -371,10 +424,11 @@
         in_specs=[pl.BlockSpec(memory_space=pltpu.SMEM), vmem, vmem],
         out_specs=(vmem, vmem),
         scratch_shapes=[pltpu.VMEM((total, rows, LANES), f32)] * 4
-        + [pltpu.VMEM((n_pre, rows, order), f32)] * 3
+        + [pltpu.VMEM((n_pre // 2, rows, order), f32)] * 4
+        + [pltpu.VMEM((n_pre, rows, order), f32)]
         + [pltpu.VMEM((order, order), t) for t in (f32, b16, f32, b16, f32, b16, b16)]
         + [dma((total,))] * 4
-        + [dma((n_pre,))] * 4,
+        + [dma((n_pre // 2,))] * 8,
         compiler_params=pltpu.CompilerParams(
             collective_id=0, has_side_effects=True, vmem_limit_bytes=40 * 1024 * 1024
         ),

time: 83.7 us -> 64.4 us (0.77)
  the two profiles are of different devices: /device:TPU:1 before, /device:TPU:0 now
where the time goes in v2:
time: 64.4 us; the launch traced here: 64 us
  Pallas kernels  58.9 us (91%)
  local copies, waits for them, and re-layouts  4.36 us (7%)
  between operations  0.65 us (1%)
    pallas_call x1, Pallas kernels, body(): pl.pallas_call(functools.partial(kernel, n_pre, n_rep), out_shape=(jax.Sh...  58.9 us
    unnamed x8, local copies, waits for them, and re-layouts  4.36 us

profile of v2, /device:TPU:0, one launch (start us, length us, event | category | flops | bytes accessed | tf_op | source)
XLA Modules:
  0.0 64.0 jit_solution(10021222724935172613)
XLA Ops:
  0.6 0.0 copy-start
  0.6 1.2 %copy-done = bf16[2,1,512,512]{3,2,1,0:T(8,128)(2,1)S(1)} copy-done((bf16[2,1,512,512]{3,2,1,0:T(8,128)(2,1)S(1)}, bf16[2,1,512,512]{3,2,1,0:T(8,128)(2,1)}, u32[]{:S(2)}) %copy-start) | copy-done | bytes 1048600
  1.9 0.0 copy-start.1
  1.9 1.0 %copy-done.1 = f32[1,2,128,512]{3,2,1,0:T(8,128)S(1)} copy-done((f32[1,2,128,512]{3,2,1,0:T(8,128)S(1)}, f32[1,2,128,512]{3,2,1,0:T(8,128)}, u32[]{:S(2)}) %copy-start.1) | copy-done | bytes 524312
  2.9 0.0 copy-start.2
  2.9 0.7 %copy-done.2 = s32[8]{0:T(128)S(1)} copy-done((s32[8]{0:T(128)S(1)}, s32[8]{0:T(128)}, u32[]{:S(2)}) %copy-start.2) | copy-done | bytes 56
  3.6 58.9 %shard_map.50 = (f32[1,2,128,512]{3,2,1,0:T(8,128)S(1)}, bf16[1,128,512]{2,1,0:T(8,128)(2,1)S(1)}) custom-call(s32[8]{0:T(128)S(1)} %copy-done.2, bf16[2,1,512,512]{3,2,1,0:T(8,128)(2,1)S(1)} %copy-done, f32[1,2,128,512]{3,2,1,0:T(8,128)S(1)} %copy-done.1), custom_call_target="tpu_custom_call" | custom-call | flops 2684354560 | bytes 4194304 | tf_op jit(solution)/shard_map/pallas_call | solution.py:418
  62.5 0.8 %copy.7 = f32[1,2,128,512]{3,2,1,0:T(8,128)} copy(f32[1,2,128,512]{3,2,1,0:T(8,128)S(1)} %get-tuple-element.4) | data formatting | bytes 1048576
  63.3 0.7 %copy.8 = bf16[1,128,512]{2,1,0:T(8,128)(2,1)} copy(bf16[1,128,512]{2,1,0:T(8,128)(2,1)S(1)} %get-tuple-element.5) | data formatting | bytes 262144
Async XLA Ops:
  0.6 1.2 %copy-start = (bf16[2,1,512,512]{3,2,1,0:T(8,128)(2,1)S(1)}, bf16[2,1,512,512]{3,2,1,0:T(8,128)(2,1)}, u32[]{:S(2)}) copy-start(bf16[2,1,512,512]{3,2,1,0:T(8,128)(2,1)} %grads_ref.1) | copy-start | bytes 3145732
  1.9 1.0 %copy-start.1 = (f32[1,2,128,512]{3,2,1,0:T(8,128)S(1)}, f32[1,2,128,512]{3,2,1,0:T(8,128)}, u32[]{:S(2)}) copy-start(f32[1,2,128,512]{3,2,1,0:T(8,128)} %state_ref.1) | copy-start | bytes 1572868
  2.9 0.7 %copy-start.2 = (s32[8]{0:T(128)S(1)}, s32[8]{0:T(128)}, u32[]{:S(2)}) copy-start(s32[8]{0:T(128)} %owner_ref.1) | copy-start | bytes 100

commit v3 on v2

--- a/solution.py
+++ b/solution.py
@@ -25,10 +25,12 @@
     n_pre,
     n_rep,
     owner_ref,
+    grads_hbm,
+    state_hbm,
+    new_state_ref,
+    update_ref,
     grads_ref,
     state_ref,
-    new_state_ref,
-    update_ref,
     loc,
     up,
     dn,
@@ -57,10 +59,11 @@
     rows_recv,
     pass_send,
     pass_recv,
+    load_sem,
 ):
     pre, rep = lax.axis_index("pre"), lax.axis_index("rep")
     shards, order = grads_ref.shape[0], grads_ref.shape[2]
-    rows, capacity = state_ref.shape[2], state_ref.shape[1]
+    rows = state_ref.shape[2]
     blocks = order // LANES
     half = n_rep // 2
     is_end = (rep == 0) | (rep == n_rep - 1)
@@ -80,7 +83,9 @@
         return other
 
     mean_tiles = [(i, j) for i in range(n_rep) for j in range(blocks)]
-    stat_tiles = [(i, j) for i in range(n_rep) for j in range(i * rows // LANES, blocks)]
+    bands_out = sorted(range(n_rep), key=lambda i: abs(2 * i + 1 - n_rep))
+    stat_tiles = [(i, j) for i in bands_out for j in range(i * rows // LANES, blocks)]
+    free = sum(0 < i < n_rep - 1 for i, _ in stat_tiles)
     early = len(mean_tiles) // 2
     after = early + len(stat_tiles)
     total = len(mean_tiles) + len(stat_tiles)
@@ -98,6 +103,24 @@
             device_id_type=pl.DeviceIdType.MESH,
         )
 
+    def load(a):
+        band = slice(a * LANES, (a + 1) * LANES)
+        return pltpu.make_async_copy(
+            grads_hbm.at[:, :, band, :], grads_ref.at[:, :, band, :], load_sem.at[a]
+        )
+
+    load_state = pltpu.make_async_copy(state_hbm, state_ref, load_sem.at[blocks])
+    load_state.start()
+    for a in range(blocks):
+        load(a).start()
+
+    count = first = second = jnp.int32(0)
+    for b in range(n_pre):
+        here = owner_ref[b] == pre
+        first = jnp.where(here & (count == 0), b, first)
+        second = jnp.where(here & (count == 1), b, second)
+        count = count + here.astype(jnp.int32)
+
     barrier = pltpu.get_barrier_semaphore()
 
     def greet(device):
@@ -157,29 +180,8 @@
         def _():
             out_copy(k).start()
 
-    for k, (i, j) in enumerate(mean_tiles):
-        r, c = slice(i * rows, (i + 1) * rows), slice(j * LANES, (j + 1) * LANES)
-        acc = grads_ref[0, 0, r, c].astype(jnp.float32)
-        for s in range(1, shards):
-            acc = acc + grads_ref[s, 0, r, c].astype(jnp.float32)
-        loc[mean_place(k)] = acc
-        if k < early:
-
-            @pl.when(is_end)
-            def _():
-                send_in(k)
-
-    def slot_of(block):
-        mine = owner_ref[block]
-
-        def count(other, found):
-            same = (owner_ref[other] == mine) & (other < block)
-            return found + same.astype(jnp.int32)
-
-        return lax.fori_loop(0, n_pre, count, jnp.int32(0))
-
     def piece(block):
-        return state_ref[0, jnp.minimum(slot_of(block), capacity - 1)]
+        return state_ref[0, ((count > 1) & (second == block)).astype(jnp.int32)]
 
     def core_copy(d):
         return remote(
@@ -195,20 +197,25 @@
             {"pre": 2 * chip_at(d) + core},
         )
 
+    load_state.wait()
     far_first = list(range(chips - 1, -1, -1))
     for d in far_first:
         core_out[d] = piece(2 * chip_at(d) + 1 - core)
         core_copy(d).start()
 
-    for a in range(blocks):
-        low = a * LANES
-        gram = nt_dot(grads_ref[0, 0, low : low + LANES, :], grads_ref[0, 0, low:, :])
+    for k, (i, j) in enumerate(mean_tiles):
+        if j == 0 and i * rows % LANES == 0:
+            load(i * rows // LANES).wait()
+        r, c = slice(i * rows, (i + 1) * rows), slice(j * LANES, (j + 1) * LANES)
+        acc = grads_ref[0, 0, r, c].astype(jnp.float32)
         for s in range(1, shards):
-            gram = gram + nt_dot(grads_ref[s, 0, low : low + LANES, :], grads_ref[s, 0, low:, :])
-        for k, (i, j) in enumerate(stat_tiles):
-            if i * rows // LANES == a:
-                r = i * rows - low
-                loc[early + k] = gram[r : r + rows, j * LANES - low : (j + 1) * LANES - low]
+            acc = acc + grads_ref[s, 0, r, c].astype(jnp.float32)
+        loc[mean_place(k)] = acc
+        if k < early:
+
+            @pl.when(is_end)
+            def _():
+                send_in(k)
 
     for d in far_first:
         block = 2 * chip_at(d) + core
@@ -221,6 +228,16 @@
         else:
             route_in[chip] = chosen
 
+    for a in range(blocks):
+        low = a * LANES
+        gram = nt_dot(grads_ref[0, 0, low : low + LANES, :], grads_ref[0, 0, low:, :])
+        for s in range(1, shards):
+            gram = gram + nt_dot(grads_ref[s, 0, low : low + LANES, :], grads_ref[s, 0, low:, :])
+        for k, (i, j) in enumerate(stat_tiles):
+            if i * rows // LANES == a:
+                r = i * rows - low
+                loc[early + k] = gram[r : r + rows, j * LANES - low : (j + 1) * LANES - low]
+
     def inject():
         for d in range(1, chips):
             route_copy(d).wait_recv()
@@ -233,9 +250,13 @@
 
     @pl.when(is_end)
     def _():
+        @pl.loop(early, early + free)
+        def _(k):
+            send_in(k)
+
         inject()
 
-        @pl.loop(early, total)
+        @pl.loop(early + free, total)
         def _(k):
             send_in(k)
 
@@ -260,9 +281,12 @@
     def pump(part, parts=10):
         left = total - after
         for k in range(left * part // parts, left * (part + 1) // parts):
-            if after + LAG + k < total:
-                step_up(after + LAG + k)
-            step_down(after + k)
+
+            @pl.when(not_end)
+            def _():
+                if after + LAG + k < total:
+                    step_up(after + LAG + k)
+                step_down(after + k)
 
     for k, (i, j) in enumerate(stat_tiles):
         stat[i * rows : (i + 1) * rows, j * LANES : (j + 1) * LANES] = tot[early + k]
@@ -370,6 +394,12 @@
     pump(9)
     pass_on(chips - 1)
 
+    @pl.when(is_end)
+    def _():
+        @pl.loop(after, total)
+        def _(k):
+            step_down(k)
+
     for k, (i, j) in enumerate(mean_tiles):
         mean[i * rows : (i + 1) * rows, j * LANES : (j + 1) * LANES] = (
             tot[mean_place(k)] / (shards * n_rep)
@@ -380,15 +410,8 @@
     for d in range(1, chips):
         pass_copy(d).wait_recv()
 
-    for j in range(capacity):
-
-        def find(block, found):
-            has, at = found
-            here = ((owner_ref[block] == pre) & (slot_of(block) == j)).astype(jnp.int32)
-            return has + here, at + here * block
-
-        has, at = lax.fori_loop(0, n_pre, find, (jnp.int32(0), jnp.int32(0)))
-        taken = jnp.full((rows, order), has, jnp.int32) > 0
+    for j, at in enumerate((first, second)):
+        taken = jnp.full((rows, order), count, jnp.int32) > j
         new_state_ref[0, j] = jnp.where(taken, rows_in[at], state_ref[0, j])
 
     for d in range(chips):
@@ -421,14 +444,17 @@
             jax.ShapeDtypeStruct(state.shape, f32),
             jax.ShapeDtypeStruct((1, rows, order), b16),
         ),
-        in_specs=[pl.BlockSpec(memory_space=pltpu.SMEM), vmem, vmem],
+        in_specs=[pl.BlockSpec(memory_space=pltpu.SMEM)]
+        + [pl.BlockSpec(memory_space=pltpu.HBM)] * 2,
         out_specs=(vmem, vmem),
-        scratch_shapes=[pltpu.VMEM((total, rows, LANES), f32)] * 4
+        scratch_shapes=[pltpu.VMEM(grads.shape, b16), pltpu.VMEM(state.shape, f32)]
+        + [pltpu.VMEM((total, rows, LANES), f32)] * 4
         + [pltpu.VMEM((n_pre // 2, rows, order), f32)] * 4
         + [pltpu.VMEM((n_pre, rows, order), f32)]
         + [pltpu.VMEM((order, order), t) for t in (f32, b16, f32, b16, f32, b16, b16)]
         + [dma((total,))] * 4
-        + [dma((n_pre // 2,))] * 8,
+        + [dma((n_pre // 2,))] * 8
+        + [dma((blocks + 1,))],
         compiler_params=pltpu.CompilerParams(
             collective_id=0, has_side_effects=True, vmem_limit_bytes=40 * 1024 * 1024
         ),

time: 64.4 us -> 61.4 us (0.953)
  Pallas kernels: 58.9 us -> 56.2 us
    pallas_call x1, Pallas kernels: 58.9 us -> 56.2 us  [body(): pl.pallas_call(functools.partial(kernel, n_pre, n_rep), out_shape=(jax.Sh...]
where the time goes in v3:
time: 61.4 us; the launch traced here: 61.2 us
  Pallas kernels  56.2 us (92%)
  local copies, waits for them, and re-layouts  4.36 us (7%)
  between operations  0.65 us (1%)
    pallas_call x1, Pallas kernels, body(): pl.pallas_call(functools.partial(kernel, n_pre, n_rep), out_shape=(jax.Sh...  56.2 us
    unnamed x8, local copies, waits for them, and re-layouts  4.36 us

profile of v3, /device:TPU:0, one launch (start us, length us, event | category | flops | bytes accessed | tf_op | source)
XLA Modules:
  0.0 61.2 jit_solution(9667657677263477360)
XLA Ops:
  0.6 0.0 copy-start
  0.6 1.2 %copy-done = bf16[2,1,512,512]{3,2,1,0:T(8,128)(2,1)S(1)} copy-done((bf16[2,1,512,512]{3,2,1,0:T(8,128)(2,1)S(1)}, bf16[2,1,512,512]{3,2,1,0:T(8,128)(2,1)}, u32[]{:S(2)}) %copy-start) | copy-done | bytes 1048600
  1.9 0.0 copy-start.1
  1.9 1.0 %copy-done.1 = f32[1,2,128,512]{3,2,1,0:T(8,128)S(1)} copy-done((f32[1,2,128,512]{3,2,1,0:T(8,128)S(1)}, f32[1,2,128,512]{3,2,1,0:T(8,128)}, u32[]{:S(2)}) %copy-start.1) | copy-done | bytes 524312
  2.9 0.0 copy-start.2
  2.9 0.7 %copy-done.2 = s32[8]{0:T(128)S(1)} copy-done((s32[8]{0:T(128)S(1)}, s32[8]{0:T(128)}, u32[]{:S(2)}) %copy-start.2) | copy-done | bytes 56
  3.6 56.2 %shard_map.50 = (f32[1,2,128,512]{3,2,1,0:T(8,128)S(1)}, bf16[1,128,512]{2,1,0:T(8,128)(2,1)S(1)}) custom-call(s32[8]{0:T(128)S(1)} %copy-done.2, bf16[2,1,512,512]{3,2,1,0:T(8,128)(2,1)S(1)} %copy-done, f32[1,2,128,512]{3,2,1,0:T(8,128)S(1)} %copy-done.1), custom_call_target="tpu_custom_call" | custom-call | flops 2684354560 | bytes 4194304 | tf_op jit(solution)/shard_map/pallas_call | solution.py:441
  59.7 0.8 %copy.7 = f32[1,2,128,512]{3,2,1,0:T(8,128)} copy(f32[1,2,128,512]{3,2,1,0:T(8,128)S(1)} %get-tuple-element.4) | data formatting | bytes 1048576
  60.5 0.7 %copy.8 = bf16[1,128,512]{2,1,0:T(8,128)(2,1)} copy(bf16[1,128,512]{2,1,0:T(8,128)(2,1)S(1)} %get-tuple-element.5) | data formatting | bytes 262144
Async XLA Ops:
  0.6 1.2 %copy-start = (bf16[2,1,512,512]{3,2,1,0:T(8,128)(2,1)S(1)}, bf16[2,1,512,512]{3,2,1,0:T(8,128)(2,1)}, u32[]{:S(2)}) copy-start(bf16[2,1,512,512]{3,2,1,0:T(8,128)(2,1)} %grads_hbm.1) | copy-start | bytes 3145732
  1.9 1.0 %copy-start.1 = (f32[1,2,128,512]{3,2,1,0:T(8,128)S(1)}, f32[1,2,128,512]{3,2,1,0:T(8,128)}, u32[]{:S(2)}) copy-start(f32[1,2,128,512]{3,2,1,0:T(8,128)} %state_hbm.1) | copy-start | bytes 1572868
  2.9 0.7 %copy-start.2 = (s32[8]{0:T(128)S(1)}, s32[8]{0:T(128)}, u32[]{:S(2)}) copy-start(s32[8]{0:T(128)} %owner_ref.1) | copy-start | bytes 100

commit v4 on v3

--- a/solution.py
+++ b/solution.py
@@ -86,7 +86,7 @@
     bands_out = sorted(range(n_rep), key=lambda i: abs(2 * i + 1 - n_rep))
     stat_tiles = [(i, j) for i in bands_out for j in range(i * rows // LANES, blocks)]
     free = sum(0 < i < n_rep - 1 for i, _ in stat_tiles)
-    early = len(mean_tiles) // 2
+    early = len(mean_tiles) * 3 // 8
     after = early + len(stat_tiles)
     total = len(mean_tiles) + len(stat_tiles)
 
@@ -180,28 +180,41 @@
         def _():
             out_copy(k).start()
 
-    def piece(block):
-        return state_ref[0, ((count > 1) & (second == block)).astype(jnp.int32)]
-
-    def core_copy(d):
+    def piece(block, j):
+        at = ((count > 1) & (second == block)).astype(jnp.int32)
+        return state_ref[0, at, :, j * LANES : (j + 1) * LANES]
+
+    def core_copy(d, j):
         return remote(
-            core_out.at[d], core_in.at[d], core_send.at[d], core_recv.at[d], {"pre": partner}
+            core_out.at[d, j],
+            core_in.at[d, j],
+            core_send.at[d, j],
+            core_recv.at[d, j],
+            {"pre": partner},
         )
 
-    def route_copy(d):
+    def route_copy(d, j):
         return remote(
-            route_out.at[d],
-            route_in.at[chip],
-            route_send.at[d],
-            route_recv.at[d],
+            route_out.at[d, j],
+            route_in.at[chip, j],
+            route_send.at[d, j],
+            route_recv.at[d, j],
             {"pre": 2 * chip_at(d) + core},
         )
 
+    def needed(j):
+        return pl.when(rep * rows < (j + 1) * LANES)
+
     load_state.wait()
     far_first = list(range(chips - 1, -1, -1))
-    for d in far_first:
-        core_out[d] = piece(2 * chip_at(d) + 1 - core)
-        core_copy(d).start()
+    columns = range(blocks - 1, -1, -1)
+    for j in columns:
+
+        @needed(j)
+        def _():
+            for d in far_first:
+                core_out[d, j] = piece(2 * chip_at(d) + 1 - core, j)
+                core_copy(d, j).start()
 
     for k, (i, j) in enumerate(mean_tiles):
         if j == 0 and i * rows % LANES == 0:
@@ -217,16 +230,22 @@
             def _():
                 send_in(k)
 
-    for d in far_first:
-        block = 2 * chip_at(d) + core
-        core_copy(d).wait_recv()
-        theirs = jnp.full((rows, order), (owner_ref[block] == partner).astype(jnp.int32)) > 0
-        chosen = jnp.where(theirs, core_in[d], piece(block))
-        if d:
-            route_out[d] = chosen
-            route_copy(d).start()
-        else:
-            route_in[chip] = chosen
+    for j in columns:
+
+        @needed(j)
+        def _():
+            for d in far_first:
+                block = 2 * chip_at(d) + core
+                core_copy(d, j).wait_recv()
+                theirs = (owner_ref[block] == partner).astype(jnp.int32)
+                chosen = jnp.where(
+                    jnp.full((rows, LANES), theirs) > 0, core_in[d, j], piece(block, j)
+                )
+                if d:
+                    route_out[d, j] = chosen
+                    route_copy(d, j).start()
+                else:
+                    route_in[chip, j] = chosen
 
     for a in range(blocks):
         low = a * LANES
@@ -239,14 +258,18 @@
                 loc[early + k] = gram[r : r + rows, j * LANES - low : (j + 1) * LANES - low]
 
     def inject():
-        for d in range(1, chips):
-            route_copy(d).wait_recv()
-        held = route_in[owner_ref[pre] // 2]
+        for j in range(blocks):
+
+            @needed(j)
+            def _():
+                for d in range(1, chips):
+                    route_copy(d, j).wait_recv()
+
         for k, (i, j) in enumerate(stat_tiles):
 
             @pl.when(rep == i)
             def _():
-                loc[early + k] = loc[early + k] + held[:, j * LANES : (j + 1) * LANES]
+                loc[early + k] = loc[early + k] + route_in[owner_ref[pre] // 2, j]
 
     @pl.when(is_end)
     def _():
@@ -273,10 +296,62 @@
     def _():
         inject()
 
-    @pl.loop(early, after + LAG)
+    start = pl.multiple_of(rep * rows, rows)
+
+    def rows_copy(d, j):
+        device = {"pre": 2 * chip_at(d) + core} if d else {"pre": partner}
+        return remote(
+            stat.at[pl.ds(start, rows), pl.ds(j * LANES, LANES)],
+            rows_in.at[pre, j],
+            rows_send.at[d, j],
+            rows_recv.at[d, j],
+            device,
+        )
+
+    def pass_copy(d, j):
+        held = rows_in.at[2 * chip_at(d) + core, j]
+        return remote(held, held, pass_send.at[d, j], pass_recv.at[d, j], {"pre": partner})
+
+    def pass_on(d, j):
+        rows_copy(d, j).wait_recv()
+        pass_copy(d, j).start()
+
+    def send_rows(j):
+        for d in far_first:
+            rows_copy(d, j).start()
+
+    @pl.loop(early, early + LAG)
     def _(k):
         step_up(k)
         step_down(k - LAG)
+
+    for k, (i, j) in enumerate(stat_tiles):
+        step_up(early + LAG + k)
+        step_down(early + k)
+        rs, cs = slice(i * rows, (i + 1) * rows), slice(j * LANES, (j + 1) * LANES)
+        stat[rs, cs] = tot[early + k]
+        if rows == LANES:
+
+            @pl.when(rep == i)
+            def _():
+                send_rows(j)
+
+            if i != j:
+                stat[cs, rs] = tot[early + k].T
+
+                @pl.when(rep == j)
+                def _():
+                    send_rows(i)
+
+    if rows != LANES:
+        for a in range(blocks):
+            for b in range(a + 1, blocks):
+                ra, rb = slice(a * LANES, (a + 1) * LANES), slice(b * LANES, (b + 1) * LANES)
+                stat[rb, ra] = stat[ra, rb].T
+        for j in range(blocks):
+            send_rows(j)
+    for j in range(blocks):
+        rows_in[pre, j] = stat[pl.ds(start, rows), j * LANES : (j + 1) * LANES]
 
     def pump(part, parts=10):
         left = total - after
@@ -288,37 +363,6 @@
                     step_up(after + LAG + k)
                 step_down(after + k)
 
-    for k, (i, j) in enumerate(stat_tiles):
-        stat[i * rows : (i + 1) * rows, j * LANES : (j + 1) * LANES] = tot[early + k]
-    for a in range(blocks):
-        for b in range(a + 1, blocks):
-            ra, rb = slice(a * LANES, (a + 1) * LANES), slice(b * LANES, (b + 1) * LANES)
-            stat[rb, ra] = stat[ra, rb].T
-
-    start = pl.multiple_of(rep * rows, rows)
-
-    def rows_copy(d):
-        device = {"pre": 2 * chip_at(d) + core} if d else {"pre": partner}
-        return remote(
-            stat.at[pl.ds(start, rows)],
-            rows_in.at[pre],
-            rows_send.at[d],
-            rows_recv.at[d],
-            device,
-        )
-
-    def pass_copy(d):
-        held = rows_in.at[2 * chip_at(d) + core]
-        return remote(held, held, pass_send.at[d], pass_recv.at[d], {"pre": partner})
-
-    def pass_on(d):
-        rows_copy(d).wait_recv()
-        pass_copy(d).start()
-
-    for d in range(1, chips):
-        rows_copy(d).start()
-    rows_copy(0).start()
-    rows_in[pre] = stat[pl.ds(start, rows), :]
     pump(0)
 
     def eye(first, count):
@@ -381,7 +425,8 @@
         pump(5 + 3 * turn)
 
     for d in range(1, chips - 1):
-        pass_on(d)
+        for j in range(blocks):
+            pass_on(d, j)
 
     @pl.loop(0, order, step=256)
     def _(b):
@@ -392,7 +437,8 @@
         last = CENTER * last + dot(last.astype(jnp.bfloat16), e_b16[...])
     precond = (1.25 * root - 0.25 * last).astype(jnp.bfloat16)
     pump(9)
-    pass_on(chips - 1)
+    for j in range(blocks):
+        pass_on(chips - 1, j)
 
     @pl.when(is_end)
     def _():
@@ -406,20 +452,31 @@
         ).astype(jnp.bfloat16)
     update_ref[0] = dot(precond, mean[...]).astype(jnp.bfloat16)
 
-    rows_copy(0).wait_recv()
-    for d in range(1, chips):
-        pass_copy(d).wait_recv()
-
-    for j, at in enumerate((first, second)):
-        taken = jnp.full((rows, order), count, jnp.int32) > j
-        new_state_ref[0, j] = jnp.where(taken, rows_in[at], state_ref[0, j])
-
-    for d in range(chips):
-        core_copy(d).wait_send()
-        rows_copy(d).wait_send()
-        if d:
-            route_copy(d).wait_send()
-            pass_copy(d).wait_send()
+    for j in range(blocks):
+        rows_copy(0, j).wait_recv()
+        for d in range(1, chips):
+            pass_copy(d, j).wait_recv()
+    for j in range(blocks):
+        cs = slice(j * LANES, (j + 1) * LANES)
+        for held, at in enumerate((first, second)):
+            taken = jnp.full((rows, LANES), count, jnp.int32) > held
+            new_state_ref[0, held, :, cs] = jnp.where(
+                taken, rows_in[at, j], state_ref[0, held, :, cs]
+            )
+
+    for j in range(blocks):
+
+        @needed(j)
+        def _():
+            for d in range(chips):
+                core_copy(d, j).wait_send()
+                if d:
+                    route_copy(d, j).wait_send()
+
+        for d in range(chips):
+            rows_copy(d, j).wait_send()
+            if d:
+                pass_copy(d, j).wait_send()
 
     @pl.loop(0, total)
     def _(k):
@@ -449,14 +506,14 @@
         out_specs=(vmem, vmem),
         scratch_shapes=[pltpu.VMEM(grads.shape, b16), pltpu.VMEM(state.shape, f32)]
         + [pltpu.VMEM((total, rows, LANES), f32)] * 4
-        + [pltpu.VMEM((n_pre // 2, rows, order), f32)] * 4
-        + [pltpu.VMEM((n_pre, rows, order), f32)]
+        + [pltpu.VMEM((n_pre // 2, blocks, rows, LANES), f32)] * 4
+        + [pltpu.VMEM((n_pre, blocks, rows, LANES), f32)]
         + [pltpu.VMEM((order, order), t) for t in (f32, b16, f32, b16, f32, b16, b16)]
         + [dma((total,))] * 4
-        + [dma((n_pre // 2,))] * 8
+        + [dma((n_pre // 2, blocks))] * 8
         + [dma((blocks + 1,))],
         compiler_params=pltpu.CompilerParams(
-            collective_id=0, has_side_effects=True, vmem_limit_bytes=40 * 1024 * 1024
+            collective_id=0, has_side_effects=True, vmem_limit_bytes=60 * 1024 * 1024
         ),
         cost_estimate=pl.CostEstimate(
             flops=20 * order**3, bytes_accessed=4 * order * order * 4, transcendentals=0

time: 61.4 us -> 59 us (0.961)
  local copies, waits for them, and re-layouts: 4.36 us -> 2.56 us
    unnamed x8 -> x4, local copies, waits for them, and re-layouts: 4.36 us -> 2.56 us
where the time goes in v4:
time: 59 us; the launch traced here: 58.8 us
  Pallas kernels  55.6 us (94%)
  local copies, waits for them, and re-layouts  2.56 us (4%)
  between operations  0.65 us (1%)
    pallas_call x1, Pallas kernels, body(): pl.pallas_call(functools.partial(kernel, n_pre, n_rep), out_shape=(jax.Sh...  55.6 us
    unnamed x4, local copies, waits for them, and re-layouts  2.56 us

profile of v4, /device:TPU:0, one launch (start us, length us, event | category | flops | bytes accessed | tf_op | source)
XLA Modules:
  0.0 58.8 jit_solution(7215742549491464841)
XLA Ops:
  0.6 55.6 %shard_map.50 = (f32[1,2,128,512]{3,2,1,0:T(8,128)}, bf16[1,128,512]{2,1,0:T(8,128)(2,1)}) custom-call(s32[8]{0:T(128)} %owner_ref.1, bf16[2,1,512,512]{3,2,1,0:T(8,128)(2,1)} %grads_hbm.1, f32[1,2,128,512]{3,2,1,0:T(8,128)} %state_hbm.1), custom_call_target="tpu_custom_call" | custom-call | flops 2684354560 | bytes 4194304 | tf_op jit(solution)/shard_map/pallas_call | solution.py:498
  56.3 0.0 copy-start
  56.3 1.9 %copy.7 = f32[1,2,128,512]{3,2,1,0:T(8,128)} copy(f32[1,2,128,512]{3,2,1,0:T(8,128)} %get-tuple-element.4) | data formatting | bytes 1048576
  58.2 0.0 copy-done
  58.2 0.7 %copy.8 = bf16[1,128,512]{2,1,0:T(8,128)(2,1)} copy(bf16[1,128,512]{2,1,0:T(8,128)(2,1)S(1)} %copy-done) | data formatting | bytes 262144
Async XLA Ops:
  56.3 1.9 %copy-start = (bf16[1,128,512]{2,1,0:T(8,128)(2,1)S(1)}, bf16[1,128,512]{2,1,0:T(8,128)(2,1)}, u32[]{:S(2)}) copy-start(bf16[1,128,512]{2,1,0:T(8,128)(2,1)} %get-tuple-element.5) | copy-start | bytes 393220

commit v5 on v4

--- a/solution.py
+++ b/solution.py
@@ -9,7 +9,7 @@
 
 DAMP = 0.05
 LANES = 128
-LAG = 3
+LAG = 2
 CENTER = 1.5625
 
 
@@ -27,7 +27,7 @@
     owner_ref,
     grads_hbm,
     state_hbm,
-    new_state_ref,
+    gain_ref,
     update_ref,
     grads_ref,
     state_ref,
@@ -180,6 +180,24 @@
         def _():
             out_copy(k).start()
 
+    def add_shards(k):
+        i, j = mean_tiles[k]
+        if j == 0 and i * rows % LANES == 0:
+            load(i * rows // LANES).wait()
+        r, c = slice(i * rows, (i + 1) * rows), slice(j * LANES, (j + 1) * LANES)
+        acc = grads_ref[0, 0, r, c].astype(jnp.float32)
+        for s in range(1, shards):
+            acc = acc + grads_ref[s, 0, r, c].astype(jnp.float32)
+        loc[mean_place(k)] = acc
+        if k < early:
+
+            @pl.when(is_end)
+            def _():
+                send_in(k)
+
+    for k in range(blocks):
+        add_shards(k)
+
     def piece(block, j):
         at = ((count > 1) & (second == block)).astype(jnp.int32)
         return state_ref[0, at, :, j * LANES : (j + 1) * LANES]
@@ -216,19 +234,8 @@
                 core_out[d, j] = piece(2 * chip_at(d) + 1 - core, j)
                 core_copy(d, j).start()
 
-    for k, (i, j) in enumerate(mean_tiles):
-        if j == 0 and i * rows % LANES == 0:
-            load(i * rows // LANES).wait()
-        r, c = slice(i * rows, (i + 1) * rows), slice(j * LANES, (j + 1) * LANES)
-        acc = grads_ref[0, 0, r, c].astype(jnp.float32)
-        for s in range(1, shards):
-            acc = acc + grads_ref[s, 0, r, c].astype(jnp.float32)
-        loc[mean_place(k)] = acc
-        if k < early:
-
-            @pl.when(is_end)
-            def _():
-                send_in(k)
+    for k in range(blocks, len(mean_tiles)):
+        add_shards(k)
 
     for j in columns:
 
@@ -363,7 +370,15 @@
                     step_up(after + LAG + k)
                 step_down(after + k)
 
+    def put_mean(k):
+        i, j = mean_tiles[k]
+        mean[i * rows : (i + 1) * rows, j * LANES : (j + 1) * LANES] = (
+            tot[mean_place(k)] / (shards * n_rep)
+        ).astype(jnp.bfloat16)
+
     pump(0)
+    for k in range(early):
+        put_mean(k)
 
     def eye(first, count):
         r = lax.broadcasted_iota(jnp.int32, (count, order), 0) + first
@@ -440,18 +455,6 @@
     for j in range(blocks):
         pass_on(chips - 1, j)
 
-    @pl.when(is_end)
-    def _():
-        @pl.loop(after, total)
-        def _(k):
-            step_down(k)
-
-    for k, (i, j) in enumerate(mean_tiles):
-        mean[i * rows : (i + 1) * rows, j * LANES : (j + 1) * LANES] = (
-            tot[mean_place(k)] / (shards * n_rep)
-        ).astype(jnp.bfloat16)
-    update_ref[0] = dot(precond, mean[...]).astype(jnp.bfloat16)
-
     for j in range(blocks):
         rows_copy(0, j).wait_recv()
         for d in range(1, chips):
@@ -460,9 +463,18 @@
         cs = slice(j * LANES, (j + 1) * LANES)
         for held, at in enumerate((first, second)):
             taken = jnp.full((rows, LANES), count, jnp.int32) > held
-            new_state_ref[0, held, :, cs] = jnp.where(
-                taken, rows_in[at, j], state_ref[0, held, :, cs]
+            gain_ref[0, held, :, cs] = jnp.where(
+                taken, rows_in[at, j] - state_ref[0, held, :, cs], 0.0
             )
+
+    for k in range(early, len(mean_tiles)):
+
+        @pl.when(is_end)
+        def _():
+            step_down(mean_place(k))
+
+        put_mean(k)
+    update_ref[0] = dot(precond, mean[...]).astype(jnp.bfloat16)
 
     for j in range(blocks):
 
@@ -495,7 +507,7 @@
     f32, b16 = jnp.float32, jnp.bfloat16
     dma = pltpu.SemaphoreType.DMA
     vmem = pl.BlockSpec(memory_space=pltpu.VMEM)
-    return pl.pallas_call(
+    gain, update = pl.pallas_call(
         functools.partial(kernel, n_pre, n_rep),
         out_shape=(
             jax.ShapeDtypeStruct(state.shape, f32),
@@ -519,6 +531,7 @@
             flops=20 * order**3, bytes_accessed=4 * order * order * 4, transcendentals=0
         ),
     )(owner, grads, state)
+    return state + gain, update
 
 
 def solution(mesh):

time: 59 us -> 59.5 us (level)
  other arithmetic: 0 us -> 1.95 us
  local copies, waits for them, and re-layouts: 2.56 us -> 0.66 us
    add x0 -> x1, other arithmetic: none -> 1.95 us  [body(): return (state + gain, update)]
    unnamed x4 -> x5, local copies, waits for them, and re-layouts: 2.56 us -> 0.66 us
where the time goes in v5:
time: 59.5 us; the launch traced here: 59.4 us
  Pallas kernels  56.1 us (94%)
  other arithmetic  1.95 us (3%)
  local copies, waits for them, and re-layouts  0.66 us (1%)
  between operations  0.66 us (1%)
    pallas_call x1, Pallas kernels, body(): pl.pallas_call(functools.partial(kernel, n_pre, n_rep), out_shape=(jax.Sh...  56.1 us
    add x1, other arithmetic, body(): return (state + gain, update)  1.95 us

profile of v5, /device:TPU:0, one launch (start us, length us, event | category | flops | bytes accessed | tf_op | source)
XLA Modules:
  0.0 59.4 jit_solution(12879666030611335499)
XLA Ops:
  0.6 0.0 copy-start
  0.6 56.1 %shard_map.50 = (f32[1,2,128,512]{3,2,1,0:T(8,128)}, bf16[1,128,512]{2,1,0:T(8,128)(2,1)}) custom-call(s32[8]{0:T(128)} %owner_ref.1, bf16[2,1,512,512]{3,2,1,0:T(8,128)(2,1)} %grads_hbm.1, f32[1,2,128,512]{3,2,1,0:T(8,128)} %state_hbm.1), custom_call_target="tpu_custom_call" | custom-call | flops 2684354560 | bytes 4194304 | tf_op jit(solution)/shard_map/pallas_call | solution.py:510
  56.8 0.0 copy-done
  56.8 0.0 copy-start.1
  56.8 1.9 %add.3 = f32[1,2,128,512]{3,2,1,0:T(8,128)} add(f32[1,2,128,512]{3,2,1,0:T(8,128)S(1)} %copy-done, f32[1,2,128,512]{3,2,1,0:T(8,128)} %get-tuple-element.4) | non-fusion elementwise | flops 131072 | bytes 1572864 | tf_op jit(solution)/shard_map/add | solution.py:534
  58.7 0.0 copy-done.1
  58.7 0.7 %copy.6 = bf16[1,128,512]{2,1,0:T(8,128)(2,1)} copy(bf16[1,128,512]{2,1,0:T(8,128)(2,1)S(1)} %copy-done.1) | data formatting | bytes 262144
Async XLA Ops:
  0.6 56.1 %copy-start = (f32[1,2,128,512]{3,2,1,0:T(8,128)S(1)}, f32[1,2,128,512]{3,2,1,0:T(8,128)}, u32[]{:S(2)}) copy-start(f32[1,2,128,512]{3,2,1,0:T(8,128)} %state_hbm.1) | copy-start | bytes 1572868
  56.8 2.0 %copy-start.1 = (bf16[1,128,512]{2,1,0:T(8,128)(2,1)S(1)}, bf16[1,128,512]{2,1,0:T(8,128)(2,1)}, u32[]{:S(2)}) copy-start(bf16[1,128,512]{2,1,0:T(8,128)(2,1)} %get-tuple-element.9) | copy-start | bytes 393220

commit v6 on v4

--- a/solution.py
+++ b/solution.py
@@ -86,7 +86,7 @@
     bands_out = sorted(range(n_rep), key=lambda i: abs(2 * i + 1 - n_rep))
     stat_tiles = [(i, j) for i in bands_out for j in range(i * rows // LANES, blocks)]
     free = sum(0 < i < n_rep - 1 for i, _ in stat_tiles)
-    early = len(mean_tiles) * 3 // 8
+    early = len(mean_tiles) // 2
     after = early + len(stat_tiles)
     total = len(mean_tiles) + len(stat_tiles)
 
@@ -513,12 +513,16 @@
         + [dma((n_pre // 2, blocks))] * 8
         + [dma((blocks + 1,))],
         compiler_params=pltpu.CompilerParams(
-            collective_id=0, has_side_effects=True, vmem_limit_bytes=60 * 1024 * 1024
+            collective_id=0, has_side_effects=True, vmem_limit_bytes=40 * 1024 * 1024
         ),
         cost_estimate=pl.CostEstimate(
             flops=20 * order**3, bytes_accessed=4 * order * order * 4, transcendentals=0
         ),
-    )(owner, grads, state)
+    )(
+        pltpu.with_memory_space_constraint(owner, pltpu.HBM),
+        pltpu.with_memory_space_constraint(grads, pltpu.HBM),
+        pltpu.with_memory_space_constraint(state, pltpu.HBM),
+    )
 
 
 def solution(mesh):

time: 59 us -> 57.1 us (0.968)
  local copies, waits for them, and re-layouts: 2.56 us -> 1.45 us
  Pallas kernels: 55.6 us -> 54.8 us
    unnamed x4 -> x2, local copies, waits for them, and re-layouts: 2.56 us -> 1.45 us
    pallas_call x1, Pallas kernels: 55.6 us -> 54.8 us  [body(): pl.pallas_call(functools.partial(kernel, n_pre, n_rep), out_shape=(jax.Sh...]
where the time goes in v6:
time: 57.1 us; the launch traced here: 56.9 us
  Pallas kernels  54.8 us (96%)
  local copies, waits for them, and re-layouts  1.45 us (3%)
  between operations  0.64 us (1%)
    pallas_call x1, Pallas kernels, body(): pl.pallas_call(functools.partial(kernel, n_pre, n_rep), out_shape=(jax.Sh...  54.8 us
    unnamed x2, local copies, waits for them, and re-layouts  1.45 us

profile of v6, /device:TPU:0, one launch (start us, length us, event | category | flops | bytes accessed | tf_op | source)
XLA Modules:
  0.0 56.9 jit_solution(18229747088616634671)
XLA Ops:
  0.6 54.8 %shard_map.50 = (f32[1,2,128,512]{3,2,1,0:T(8,128)S(1)}, bf16[1,128,512]{2,1,0:T(8,128)(2,1)S(1)}) custom-call(s32[8]{0:T(128)} %owner_ref.1, bf16[2,1,512,512]{3,2,1,0:T(8,128)(2,1)} %grads_hbm.1, f32[1,2,128,512]{3,2,1,0:T(8,128)} %state_hbm.1), custom_call_target="tpu_custom_call" | custom-call | flops 2684354560 | bytes 4194304 | tf_op jit(solution)/shard_map/pallas_call | solution.py:498
  55.5 0.8 %copy.7 = f32[1,2,128,512]{3,2,1,0:T(8,128)} copy(f32[1,2,128,512]{3,2,1,0:T(8,128)S(1)} %get-tuple-element.4) | data formatting | bytes 1048576
  56.3 0.7 %copy.8 = bf16[1,128,512]{2,1,0:T(8,128)(2,1)} copy(bf16[1,128,512]{2,1,0:T(8,128)(2,1)S(1)} %get-tuple-element.5) | data formatting | bytes 262144
